TPU v7x, 32 devices: a whole 2x2x4 slice. The times are simulated.
32 devices in a mesh: seq: 4 (over y, core), fsdp: 8 (over z, x).
Axes of the slice: x: 2, y: 2, z: 4, core: 2. Of those that a mesh axis runs over, the one named last changes fastest.
Arguments:
- frames_in: bfloat16 [8, 1024, 768], P('fsdp', 'seq'), may hold values from -6 to 6
- norm1_gain: bfloat16 [2, 768], P(None, 'fsdp'), may hold values from 0.25 to 1.75
- norm1_bias: bfloat16 [2, 768], P(None, 'fsdp'), may hold values from -3 to 3
- qkv_weight: bfloat16 [2, 768, 2304], P(None, 'fsdp'), may hold values from -0.3125 to 0.3125
- qv_bias: bfloat16 [2, 2, 768], P(None, None, 'fsdp'), may hold values from -0.59765625 to 0.59765625
- out_weight: bfloat16 [2, 768, 768], P(None, 'fsdp'), may hold values from -0.21875 to 0.21875
- out_bias: bfloat16 [2, 768], P(None, 'fsdp'), may hold values from -3 to 3
- norm2_gain: bfloat16 [2, 768], P(None, 'fsdp'), may hold values from 0.25 to 1.75
- norm2_bias: bfloat16 [2, 768], P(None, 'fsdp'), may hold values from -3 to 3
- fc1_weight: bfloat16 [2, 768, 3072], P(None, 'fsdp'), may hold values from -0.21875 to 0.21875
- fc1_bias: bfloat16 [2, 3072], P(None, 'fsdp'), may hold values from -3 to 3
- fc2_weight: bfloat16 [2, 3072, 768], P(None, 'fsdp'), may hold values from -0.109375 to 0.109375
- fc2_bias: bfloat16 [2, 768], P(None, 'fsdp'), may hold values from -3 to 3
- out_cotangent: bfloat16 [8, 1024, 768], P('fsdp', 'seq'), may hold values from -6 to 6
Outputs:
- frames_out: bfloat16 [8, 1024, 768], P('fsdp', 'seq')
- frames_grad: float32 [8, 1024, 768], P('fsdp', 'seq')
- norm1_gain_grad: float32 [2, 768], P(None, 'fsdp')
- norm1_bias_grad: float32 [2, 768], P(None, 'fsdp')
- qkv_weight_grad: float32 [2, 768, 2304], P(None, 'fsdp')
- qv_bias_grad: float32 [2, 2, 768], P(None, None, 'fsdp')
- out_weight_grad: float32 [2, 768, 768], P(None, 'fsdp')
- out_bias_grad: float32 [2, 768], P(None, 'fsdp')
- norm2_gain_grad: float32 [2, 768], P(None, 'fsdp')
- norm2_bias_grad: float32 [2, 768], P(None, 'fsdp')
- fc1_weight_grad: float32 [2, 768, 3072], P(None, 'fsdp')
- fc1_bias_grad: float32 [2, 3072], P(None, 'fsdp')
- fc2_weight_grad: float32 [2, 3072, 768], P(None, 'fsdp')
- fc2_bias_grad: float32 [2, 768], P(None, 'fsdp')
All inputs are finite; a program needn't handle non-finite values.
Results may differ from a plain program's by a relative error of at most 0.023.
Values may be sent and summed in bfloat16 or wider, within the bound.
A program may use at most 192 MiB of HBM per device.

v0:
```python
from functools import partial
import math
import jax
import jax.numpy as jnp
from jax import lax
from jax.sharding import PartitionSpec as P

D = 768
HEADS = 12
HEAD_DIM = 64
EPSILON = 1e-05


def norm_rows(values, gain, shift):
    center = jnp.mean(values, axis=-1, keepdims=True)
    centred = values - center
    spread = jnp.mean(centred * centred, axis=-1, keepdims=True)
    return centred * lax.rsqrt(spread + EPSILON) * gain + shift


def qkv_shift(pair_bias):
    query_part = pair_bias[0].reshape(HEADS, 1, HEAD_DIM)
    value_part = pair_bias[1].reshape(HEADS, 1, HEAD_DIM)
    joined = jnp.concatenate([query_part, jnp.zeros_like(query_part), value_part], axis=1)
    return joined.reshape(3 * D)


BF = jnp.bfloat16
F32 = jnp.float32


def seq_gather(block):
    return lax.all_gather(block, "seq", axis=1, tiled=True)


def seq_reduce(partial_sum):
    summed = lax.psum_scatter(partial_sum.astype(BF), "seq", scatter_dimension=1, tiled=True)
    return summed.astype(F32)


def dot_in(rows, matrix):
    return jnp.einsum("cfi,io->cfo", rows, matrix, preferred_element_type=F32)


def dot_back(rows, matrix):
    return jnp.einsum("cfo,io->cfi", rows, matrix, preferred_element_type=F32)


def dot_grad(left, right):
    return jnp.einsum("cfi,cfo->io", left, right, preferred_element_type=F32)


def take_part(array, axis, parts, index):
    size = array.shape[axis] // parts
    return lax.dynamic_slice_in_dim(array, index * size, size, axis)


def put_part(part, axis, parts, index):
    shape = list(part.shape)
    shape[axis] = shape[axis] * parts
    return lax.dynamic_update_slice_in_dim(
        jnp.zeros(shape, part.dtype), part, index * part.shape[axis], axis
    )


def layer_forward(stream, weights):
    (
        gain_one,
        shift_one,
        w_qkv,
        qkv_add,
        w_out,
        out_shift,
        gain_two,
        shift_two,
        w_up,
        up_shift,
        w_down,
        down_shift,
    ) = weights
    normed_one = seq_gather(norm_rows(stream, gain_one, shift_one).astype(BF))
    heads = (dot_in(normed_one, w_qkv) + qkv_add).astype(BF)
    outs = [attend_forward(heads[clip]) for clip in range(heads.shape[0])]
    mixed = jnp.stack([pair[0] for pair in outs])
    log_total = jnp.stack([pair[1] for pair in outs])
    attended = stream + (seq_reduce(dot_in(mixed, w_out)) + out_shift)
    normed_two = seq_gather(norm_rows(attended, gain_two, shift_two).astype(BF))
    hidden = dot_in(normed_two, w_up) + up_shift
    activated = jax.nn.gelu(hidden, approximate=False).astype(BF)
    result = attended + (seq_reduce(dot_in(activated, w_down)) + down_shift)
    return (
        (stream, normed_one, heads, log_total, mixed, attended, normed_two, hidden, activated),
        result,
    )


def sum_rows(rows):
    return jnp.sum(rows.astype(F32), axis=(0, 1))


def layer_backward(upstream, weights, state, seq_index, seq_size, fsdp_size):
    (
        gain_one,
        shift_one,
        w_qkv,
        qkv_add,
        w_out,
        out_shift,
        gain_two,
        shift_two,
        w_up,
        up_shift,
        w_down,
        down_shift,
    ) = weights
    stream, normed_one, heads, log_total, mixed, attended, normed_two, hidden, activated = state
    grad_down_local = upstream.astype(BF)
    down_shift_grad = sum_rows(grad_down_local)
    grad_down = seq_gather(grad_down_local)
    w_down_grad = dot_grad(activated, grad_down)
    grad_active = dot_back(grad_down, w_down)
    gelu_pull = jax.vjp(partial(jax.nn.gelu, approximate=False), hidden)[1]
    grad_hidden = gelu_pull(grad_active)[0].astype(BF)
    up_shift_grad = sum_rows(grad_hidden)
    w_up_grad = dot_grad(normed_two, grad_hidden)
    grad_normed_two = seq_reduce(dot_back(grad_hidden, w_up))
    _, pull_two = jax.vjp(norm_rows, attended, gain_two, shift_two)
    grad_attended, gain_two_grad, shift_two_grad = pull_two(grad_normed_two)
    grad_attended = grad_attended + upstream
    grad_out_local = grad_attended.astype(BF)
    out_shift_grad = sum_rows(grad_out_local)
    grad_out = seq_gather(grad_out_local)
    w_out_grad = dot_grad(mixed, grad_out)
    grad_mixed = dot_back(grad_out, w_out).astype(BF)
    grad_projected = jnp.stack(
        [
            attend_backward((heads[clip], log_total[clip], grad_mixed[clip]))
            for clip in range(heads.shape[0])
        ]
    )
    qkv_add_grad = sum_rows(grad_projected)
    w_qkv_grad = dot_grad(normed_one, grad_projected)
    grad_normed_one = seq_reduce(dot_back(grad_projected, w_qkv))
    _, pull_one = jax.vjp(norm_rows, stream, gain_one, shift_one)
    grad_stream, gain_one_grad, shift_one_grad = pull_one(grad_normed_one)
    grad_stream = grad_stream + grad_attended
    out_columns = lax.all_to_all(
        w_out_grad.astype(BF), "seq", split_axis=1, concat_axis=0, tiled=True
    )
    big = jnp.concatenate(
        [w_up_grad.astype(BF), w_down_grad.astype(BF), w_qkv_grad.astype(BF), out_columns], axis=1
    )
    local_heads = qkv_add_grad.shape[0] // (3 * HEAD_DIM)
    triple = qkv_add_grad.reshape(local_heads, 3, HEAD_DIM)
    up_parts = put_part(up_shift_grad.reshape(fsdp_size, -1), 1, seq_size, seq_index)
    small = jnp.concatenate(
        [
            gain_one_grad,
            shift_one_grad,
            put_part(triple[:, 0].reshape(-1), 0, seq_size, seq_index),
            put_part(triple[:, 2].reshape(-1), 0, seq_size, seq_index),
            out_shift_grad,
            gain_two_grad,
            shift_two_grad,
            down_shift_grad,
            up_parts.reshape(-1),
        ]
    )
    return (grad_stream, big, small)


def reduce_big(big):
    owned = lax.psum_scatter(big, "fsdp", scatter_dimension=0, tiled=True)
    return lax.all_gather(owned, "seq", axis=0, tiled=False)


def unpack_big(gathered, sizes):
    up, down, qkv, out = sizes
    spots = [0, up, up + down, up + down + qkv, up + down + qkv + out]
    rows = gathered.shape[1]
    members = [gathered[:, :, spots[i] : spots[i + 1]].astype(F32) for i in range(4)]
    fsdp_size = D // rows
    seq_size = gathered.shape[0]
    w_up = members[0].reshape(seq_size, rows, fsdp_size, -1).transpose(1, 2, 0, 3).reshape(rows, -1)
    w_down = members[1].reshape(seq_size * rows, -1)
    w_qkv = members[2].transpose(1, 0, 2).reshape(rows, -1)
    w_out = members[3].transpose(1, 0, 2).reshape(rows, -1)
    return (w_qkv, w_out, w_up, w_down)


def attend_forward(packed):
    frames = packed.shape[0]
    local_heads = packed.shape[1] // (3 * HEAD_DIM)
    parts = packed.reshape(frames, local_heads, 3, HEAD_DIM)
    scores = jnp.einsum(
        "qhd,khd->hqk", parts[:, :, 0], parts[:, :, 1], preferred_element_type=jnp.float32
    ) * HEAD_DIM ** (-0.5)
    peak_score = jnp.max(scores, axis=-1, keepdims=True)
    expanded = jnp.exp(scores - peak_score)
    totals = jnp.sum(expanded, axis=-1, keepdims=True)
    weights = (expanded / totals).astype(jnp.bfloat16)
    mixed = jnp.einsum("hqk,khd->qhd", weights, parts[:, :, 2], preferred_element_type=jnp.float32)
    return (
        mixed.reshape(frames, local_heads * HEAD_DIM).astype(jnp.bfloat16),
        (peak_score + jnp.log(totals))[..., 0],
    )


def attend_backward(inputs):
    packed, log_total, incoming = inputs
    frames = packed.shape[0]
    local_heads = packed.shape[1] // (3 * HEAD_DIM)
    parts = packed.reshape(frames, local_heads, 3, HEAD_DIM)
    queries = parts[:, :, 0]
    keys_local = parts[:, :, 1]
    values_local = parts[:, :, 2]
    scale = HEAD_DIM ** (-0.5)
    scores = (
        jnp.einsum("qhd,khd->hqk", queries, keys_local, preferred_element_type=jnp.float32) * scale
    )
    probs = jnp.exp(scores - log_total[..., None])
    incoming_heads = incoming.reshape(frames, local_heads, HEAD_DIM)
    grad_probs = jnp.einsum(
        "qhd,khd->hqk", incoming_heads, values_local, preferred_element_type=jnp.float32
    )
    grad_values = jnp.einsum(
        "hqk,qhd->khd",
        probs.astype(jnp.bfloat16),
        incoming_heads,
        preferred_element_type=jnp.float32,
    )
    grad_scores = (
        probs * (grad_probs - jnp.sum(probs * grad_probs, axis=-1, keepdims=True))
    ).astype(jnp.bfloat16)
    grad_queries = (
        jnp.einsum("hqk,khd->qhd", grad_scores, keys_local, preferred_element_type=jnp.float32)
        * scale
    )
    grad_keys = (
        jnp.einsum("hqk,qhd->khd", grad_scores, queries, preferred_element_type=jnp.float32) * scale
    )
    stacked = jnp.stack([grad_queries, grad_keys, grad_values], axis=2)
    return stacked.reshape(frames, local_heads * 3 * HEAD_DIM).astype(jnp.bfloat16)


def local(
    frames_in,
    norm1_gain,
    norm1_bias,
    qkv_weight,
    qv_bias,
    out_weight,
    out_bias,
    norm2_gain,
    norm2_bias,
    fc1_weight,
    fc1_bias,
    fc2_weight,
    fc2_bias,
    out_cotangent,
):
    shards = (
        norm1_gain,
        norm1_bias,
        qkv_weight,
        qv_bias,
        out_weight,
        out_bias,
        norm2_gain,
        norm2_bias,
        fc1_weight,
        fc1_bias,
        fc2_weight,
        fc2_bias,
    )
    layer_count = qkv_weight.shape[0]
    fsdp_size = lax.axis_size("fsdp")
    seq_size = lax.axis_size("seq")
    seq_index = lax.axis_index("seq")
    owner = lax.axis_index("fsdp")
    rows = qkv_weight.shape[1]
    part_rows = fc1_bias.shape[1] // seq_size
    hidden_local = fsdp_size * part_rows
    small_in = jnp.concatenate(
        [
            norm1_gain,
            norm1_bias,
            qv_bias[:, 0],
            qv_bias[:, 1],
            out_bias,
            norm2_gain,
            norm2_bias,
            fc2_bias,
            fc1_bias,
        ],
        axis=1,
    )
    small_all = lax.all_gather(small_in.reshape(-1), "fsdp", axis=0, tiled=False)
    small_all = small_all.reshape(fsdp_size, layer_count, -1).astype(F32)
    weights = []
    for level in range(layer_count):
        up_part = take_part(fc1_weight[level].reshape(rows, fsdp_size, -1), 2, seq_size, seq_index)
        packed = jnp.concatenate(
            [
                up_part.reshape(rows, hidden_local),
                take_part(fc2_weight[level], 0, seq_size, seq_index),
                take_part(qkv_weight[level], 1, seq_size, seq_index),
                out_weight[level],
            ],
            axis=1,
        )
        packed = lax.all_gather(packed, "fsdp", axis=0, tiled=True)
        third = 3 * D // seq_size
        w_up = packed[:, :hidden_local]
        w_down = packed[:, hidden_local : hidden_local + D]
        w_qkv = packed[:, hidden_local + D : hidden_local + D + third]
        w_out = take_part(packed[:, hidden_local + D + third :], 0, seq_size, seq_index)
        pieces = small_all[:, level]
        vectors = [pieces[:, i * rows : (i + 1) * rows].reshape(D) for i in range(8)]
        gain_one, shift_one, query_add, value_add, out_shift, gain_two, shift_two, down_shift = (
            vectors
        )
        up_shift = take_part(pieces[:, 8 * rows :], 1, seq_size, seq_index).reshape(hidden_local)
        qkv_add = take_part(qkv_shift(jnp.stack([query_add, value_add])), 0, seq_size, seq_index)
        weights.append(
            (
                gain_one,
                shift_one,
                w_qkv,
                qkv_add,
                w_out,
                out_shift,
                gain_two,
                shift_two,
                w_up,
                up_shift,
                w_down,
                down_shift,
            )
        )
    stream = frames_in.astype(F32)
    saved = []
    for level in range(layer_count):
        kept, stream = layer_forward(stream, weights[level])
        saved.append(kept)
    frames_out = stream.astype(BF)
    upstream = out_cotangent.astype(F32)
    reduced = [None] * layer_count
    smalls = [None] * layer_count
    for level in reversed(range(layer_count)):
        upstream, big, small = layer_backward(
            upstream, weights[level], saved[level], seq_index, seq_size, fsdp_size
        )
        smalls[level] = small
        reduced[level] = unpack_big(
            reduce_big(big), (hidden_local, D, 3 * D // seq_size, D // seq_size)
        )
    small_sum = lax.psum(jnp.stack(smalls), ("seq", "fsdp"))
    vectors = [take_part(small_sum[:, i * D : (i + 1) * D], 1, fsdp_size, owner) for i in range(8)]
    up_sum = take_part(small_sum[:, 8 * D :], 1, fsdp_size, owner)
    qkv_grad, out_grad, up_grad, down_grad = [
        jnp.stack([reduced[level][member] for level in range(layer_count)]) for member in range(4)
    ]
    return (
        frames_out,
        upstream,
        vectors[0],
        vectors[1],
        qkv_grad,
        jnp.stack([vectors[2], vectors[3]], axis=1),
        out_grad,
        vectors[4],
        vectors[5],
        vectors[6],
        up_grad,
        up_sum,
        down_grad,
        vectors[7],
    )


def solution(mesh):
    in_specs = (
        P("fsdp", "seq", None),
        P(None, "fsdp"),
        P(None, "fsdp"),
        P(None, "fsdp", None),
        P(None, None, "fsdp"),
        P(None, "fsdp", None),
        P(None, "fsdp"),
        P(None, "fsdp"),
        P(None, "fsdp"),
        P(None, "fsdp", None),
        P(None, "fsdp"),
        P(None, "fsdp", None),
        P(None, "fsdp"),
        P("fsdp", "seq", None),
    )
    out_specs = (
        P("fsdp", "seq", None),
        P("fsdp", "seq", None),
        P(None, "fsdp"),
        P(None, "fsdp"),
        P(None, "fsdp", None),
        P(None, None, "fsdp"),
        P(None, "fsdp", None),
        P(None, "fsdp"),
        P(None, "fsdp"),
        P(None, "fsdp"),
        P(None, "fsdp", None),
        P(None, "fsdp"),
        P(None, "fsdp", None),
        P(None, "fsdp"),
    )
    return jax.shard_map(local, mesh=mesh, in_specs=in_specs, out_specs=out_specs, check_vma=False)
```

profile of v0, /device:TPU:0, one launch (start us, length us, event | category | flops | bytes accessed | tf_op | source)
XLA Modules:
  0.0 1093.3 jit_solution(3094065393402558453)
XLA Ops:
  11.4 32.3 %all-gather.2 = bf16[8,1,2304]{2,1,0:T(2,128)(2,1)S(1)} all-gather(bf16[1,1,2304]{2,1,0:T(2,128)(2,1)S(1)} %reshape.700), channel_id=1, replica_groups=mesh['seq'=4,'fsdp'=8] {'fsdp'}, dimensions={0}, use_global_device_ids=true | all-gather | bytes 41472 | tf_op jit(solution)/shard_map/all_gather | solution.py:298
  51.9 15.1 %all-gather.16.cloned.1.call-done = bf16[1,1024,768]{2,1,0:T(8,128)(2,1)} async-done(((bf16[1,256,768]{2,1,0:T(8,128)(2,1)}), bf16[1,1024,768]{2,1,0:T(8,128)(2,1)}) %all-gather.16.cloned.1.call-update) | async-done | bytes 1572880 | tf_op jit(solution)/shard_map/all_gather | solution.py:33
  67.1 80.3 %all-gather.18.cloned.1.call-done = bf16[768,2880]{1,0:T(8,128)(2,1)} async-done(((bf16[96,2880]{1,0:T(8,128)(2,1)}), bf16[768,2880]{1,0:T(8,128)(2,1)}) %all-gather.18.cloned.1.call-update) | async-done | bytes 4423696 | tf_op jit(solution)/shard_map/all_gather | solution.py:312
  147.3 2.8 add_convert_fusion.2
  154.1 2.5 copy-done
  156.5 2.6 fusion.103
  164.3 26.2 %reduce-scatter.15.cloned.1.call-done = bf16[1,256,768]{2,1,0:T(8,128)(2,1)} async-done(((bf16[1,1024,768]{2,1,0:T(8,128)(2,1)}), bf16[1,256,768]{2,1,0:T(8,128)(2,1)}) %reduce-scatter.15.cloned.1.call-update) | async-done | bytes 393232 | tf_op jit(solution)/shard_map/reduce_scatter | solution.py:37
  195.7 19.1 %all-gather.20.cloned.1.call-done = bf16[1,1024,768]{2,1,0:T(8,128)(2,1)} async-done(((bf16[1,256,768]{2,1,0:T(8,128)(2,1)}), bf16[1,1024,768]{2,1,0:T(8,128)(2,1)}) %all-gather.20.cloned.1.call-update) | async-done | bytes 1572880 | tf_op jit(solution)/shard_map/all_gather | solution.py:33
  214.9 11.4 %multiply_convert_fusion.3 = (bf16[1024,768]{1,0:T(8,128)(2,1)S(1)}, f32[1024,768]{1,0:T(8,128)}, f32[1024,768]{1,0:T(8,128)}) fusion(f32[768]{0:T(1024)S(1)} %add.284, bf16[768,2880]{1,0:T(8,128)(2,1)} %all-gather.18.cloned.1.call-done, bf16[1,1024,768]{2,1,0:T(8,128)(2,1)} %all-gather.20.cloned.1.call-done), kind=kOutput, calls=%fused_computation.51 | convolution fusion | flops 1259864064 | bytes 10619904 | tf_op jit(solution)/shard_map/cfi,io->cfo/dot_general | solution.py:42
  227.5 3.8 fusion.73
  234.1 25.5 %reduce-scatter.17.cloned.1.call-done = bf16[1,256,768]{2,1,0:T(8,128)(2,1)} async-done(((bf16[1,1024,768]{2,1,0:T(8,128)(2,1)}), bf16[1,256,768]{2,1,0:T(8,128)(2,1)}) %reduce-scatter.17.cloned.1.call-update) | async-done | bytes 393232 | tf_op jit(solution)/shard_map/reduce_scatter | solution.py:37
  262.6 77.1 %all-gather.24.cloned.1.call-done = bf16[768,2880]{1,0:T(8,128)(2,1)} async-done(((bf16[96,2880]{1,0:T(8,128)(2,1)}), bf16[768,2880]{1,0:T(8,128)(2,1)}) %all-gather.24.cloned.1.call-update) | async-done | bytes 4423696 | tf_op jit(solution)/shard_map/all_gather | solution.py:312
  341.6 18.1 %all-gather.22.cloned.1.call-done = bf16[1,1024,768]{2,1,0:T(8,128)(2,1)} async-done(((bf16[1,256,768]{2,1,0:T(8,128)(2,1)}), bf16[1,1024,768]{2,1,0:T(8,128)(2,1)}) %all-gather.22.cloned.1.call-update) | async-done | bytes 1572880 | tf_op jit(solution)/shard_map/all_gather | solution.py:33
  359.7 2.8 add_convert_fusion.1
  366.5 2.5 copy-done.1
  369.0 2.6 fusion.102
  374.5 28.1 %reduce-scatter.19.cloned.1.call-done = bf16[1,256,768]{2,1,0:T(8,128)(2,1)} async-done(((bf16[1,1024,768]{2,1,0:T(8,128)(2,1)}), bf16[1,256,768]{2,1,0:T(8,128)(2,1)}) %reduce-scatter.19.cloned.1.call-update) | async-done | bytes 393232 | tf_op jit(solution)/shard_map/reduce_scatter | solution.py:37
  405.9 18.8 %all-gather.26.cloned.1.call-done = bf16[1,1024,768]{2,1,0:T(8,128)(2,1)} async-done(((bf16[1,256,768]{2,1,0:T(8,128)(2,1)}), bf16[1,1024,768]{2,1,0:T(8,128)(2,1)}) %all-gather.26.cloned.1.call-update) | async-done | bytes 1572880 | tf_op jit(solution)/shard_map/all_gather | solution.py:33
  424.7 11.6 %multiply_convert_fusion.2 = (bf16[1024,768]{1,0:T(8,128)(2,1)}, f32[1024,768]{1,0:T(8,128)}, f32[1024,768]{1,0:T(8,128)}) fusion(f32[768]{0:T(1024)S(1)} %add.305, bf16[768,2880]{1,0:T(8,128)(2,1)} %all-gather.24.cloned.1.call-done, bf16[1,1024,768]{2,1,0:T(8,128)(2,1)} %all-gather.26.cloned.1.call-done), kind=kOutput, calls=%fused_computation.38 | convolution fusion | flops 1259864064 | bytes 10619904 | tf_op jit(solution)/shard_map/cfi,io->cfo/dot_general | solution.py:42
  436.4 9.6 all-gather.28.cloned.1.call-done
  445.9 6.4 convert_reduce_fusion
  453.5 3.8 fusion.76
  457.4 4.3 fusion.75
  461.9 23.8 %reduce-scatter.23.cloned.1.call-done = bf16[1,256,768]{2,1,0:T(8,128)(2,1)} async-done(((bf16[1,1024,768]{2,1,0:T(8,128)(2,1)}), bf16[1,256,768]{2,1,0:T(8,128)(2,1)}) %reduce-scatter.23.cloned.1.call-update) | async-done | bytes 393232 | tf_op jit(solution)/shard_map/reduce_scatter | solution.py:37
  488.2 28.7 %reduce-scatter.21.cloned.1.call-done = bf16[1,256,768]{2,1,0:T(8,128)(2,1)} async-done(((bf16[1,1024,768]{2,1,0:T(8,128)(2,1)}), bf16[1,256,768]{2,1,0:T(8,128)(2,1)}) %reduce-scatter.21.cloned.1.call-update) | async-done | bytes 393232 | tf_op jit(solution)/shard_map/reduce_scatter | solution.py:37
  521.9 18.6 %all-gather.30.cloned.1.call-done = bf16[1,1024,768]{2,1,0:T(8,128)(2,1)} async-done(((bf16[1,256,768]{2,1,0:T(8,128)(2,1)}), bf16[1,1024,768]{2,1,0:T(8,128)(2,1)}) %all-gather.30.cloned.1.call-update) | async-done | bytes 1572880 | tf_op jit(solution)/shard_map/all_gather | solution.py:33
  542.6 7.0 fusion.93
  549.6 6.6 multiply_reduce_fusion.1
  556.8 5.3 multiply_convert_fusion.1
  562.1 5.1 fusion.88
  571.4 3.9 fusion.78
  575.3 28.3 %reduce-scatter.25.cloned.1.call-done = bf16[1,256,768]{2,1,0:T(8,128)(2,1)} async-done(((bf16[1,1024,768]{2,1,0:T(8,128)(2,1)}), bf16[1,256,768]{2,1,0:T(8,128)(2,1)}) %reduce-scatter.25.cloned.1.call-update) | async-done | bytes 393232 | tf_op jit(solution)/shard_map/reduce_scatter | solution.py:37
  607.5 2.8 convert_reduce_fusion.11
  610.5 19.6 %all-gather.32.cloned.1.call-done = bf16[1,1024,768]{2,1,0:T(8,128)(2,1)} async-done(((bf16[1,256,768]{2,1,0:T(8,128)(2,1)}), bf16[1,1024,768]{2,1,0:T(8,128)(2,1)}) %all-gather.32.cloned.1.call-update) | async-done | bytes 1572880 | tf_op jit(solution)/shard_map/all_gather | solution.py:33
  630.1 6.4 convert_reduce_fusion.1
  637.7 3.9 fusion.77
  641.7 28.3 %reduce-scatter.27.cloned.1.call-done = bf16[1,256,768]{2,1,0:T(8,128)(2,1)} async-done(((bf16[1,1024,768]{2,1,0:T(8,128)(2,1)}), bf16[1,256,768]{2,1,0:T(8,128)(2,1)}) %reduce-scatter.27.cloned.1.call-update) | async-done | bytes 393232 | tf_op jit(solution)/shard_map/reduce_scatter | solution.py:37
  674.1 2.7 convert_reduce_fusion.12
  676.9 3.5 fusion.66
  680.4 2.5 fusion.63
  684.3 3.5 all-to-all-start.1
  687.8 3.8 fusion.83
  691.6 7.7 all-to-all-done.1
  700.0 3.2 pad_maximum_fusion.1
  703.2 5.8 copy.193
  711.9 7.2 multiply_reduce_fusion
  720.5 5.3 multiply_convert_fusion
  725.8 5.0 fusion.86
  736.3 3.8 fusion.79
  740.2 3.5 fusion.69
  743.7 2.5 fusion.60
  747.6 3.5 all-to-all-start
  751.3 3.8 fusion.80
  755.1 3.4 all-to-all-done
  759.2 3.2 pad_maximum_fusion
  762.4 5.8 copy.191
  770.2 18.1 %reduce-scatter.33.cloned.1.call-done = bf16[96,2304]{1,0:T(8,128)(2,1)} async-done(((bf16[768,2304]{1,0:T(8,128)(2,1)}), bf16[96,2304]{1,0:T(8,128)(2,1)}) %reduce-scatter.33.cloned.1.call-update) | async-done | bytes 442384 | tf_op jit(solution)/shard_map/reduce_scatter | solution.py:173
  789.0 30.4 %reduce-scatter.29.cloned.1.call-done = bf16[1,256,768]{2,1,0:T(8,128)(2,1)} async-done(((bf16[1,1024,768]{2,1,0:T(8,128)(2,1)}), bf16[1,256,768]{2,1,0:T(8,128)(2,1)}) %reduce-scatter.29.cloned.1.call-update) | async-done | bytes 393232 | tf_op jit(solution)/shard_map/reduce_scatter | solution.py:37
  823.1 78.7 %reduce-scatter.31.cloned.1.call-done = bf16[96,2304]{1,0:T(8,128)(2,1)} async-done(((bf16[768,2304]{1,0:T(8,128)(2,1)}), bf16[96,2304]{1,0:T(8,128)(2,1)}) %reduce-scatter.31.cloned.1.call-update) | async-done | bytes 442384 | tf_op jit(solution)/shard_map/reduce_scatter | solution.py:173
  901.8 21.9 %all-gather.38.cloned.1.call-done = bf16[384,2304]{1,0:T(8,128)(2,1)} async-done(((bf16[96,2304]{1,0:T(8,128)(2,1)}), bf16[384,2304]{1,0:T(8,128)(2,1)}) %all-gather.38.cloned.1.call-update) | async-done | bytes 1769488 | tf_op jit(solution)/shard_map/all_gather | solution.py:174
  934.5 2.5 stack_reshape.37
  938.7 109.0 %all-reduce.2.cloned.1.call-done = f32[2,9216]{1,0:T(2,128)} async-done(((f32[2,9216]{1,0:T(2,128)}), f32[2,9216]{1,0:T(2,128)}) %all-reduce.2.cloned.1.call-update) | async-done | bytes 73744 | tf_op jit(solution)/shard_map/psum | solution.py:358
  1054.3 17.6 %all-gather.36.cloned.1.call-done = bf16[384,2304]{1,0:T(8,128)(2,1)} async-done(((bf16[96,2304]{1,0:T(8,128)(2,1)}), bf16[384,2304]{1,0:T(8,128)(2,1)}) %all-gather.36.cloned.1.call-update) | async-done | bytes 1769488 | tf_op jit(solution)/shard_map/all_gather | solution.py:174
  1080.9 2.5 maximum_convert_fusion.4
  (430 shorter events, 121.4 us)
Async XLA Ops:
  7.2 39.2 %copy-start.21 = (bf16[2,96,3072]{2,1,0:T(8,128)(2,1)S(1)}, bf16[2,96,3072]{2,1,0:T(8,128)(2,1)}, u32[]{:S(2)}) copy-start(bf16[2,96,3072]{2,1,0:T(8,128)(2,1)} %param.23) | copy-start | bytes 3538948
  7.2 59.9 %all-gather.16.cloned.1.call-start = ((), (), s32[]{:S(2)}) async-start(), calls=%async_computation.12 | async-start | bytes 1966080 | tf_op jit(solution)/shard_map/all_gather | solution.py:33
  8.5 38.5 %copy-start.42 = (f32[256]{0:T(256)}, f32[256]{0:T(256)S(1)}, u32[]{:S(2)}) copy-start(f32[256]{0:T(256)S(1)} %broadcast_multiply_fusion.3) | copy-start | bytes 3076
  9.7 39.2 %copy-start.52 = (f32[256]{0:T(256)}, f32[256]{0:T(256)S(1)}, u32[]{:S(2)}) copy-start(f32[256]{0:T(256)S(1)} %fusion.162) | copy-start | bytes 3076
  46.3 101.0 %all-gather.18.cloned.1.call-start = ((), (), s32[]{:S(2)}) async-start(), calls=%async_computation.13 | async-start | bytes 5087232 | tf_op jit(solution)/shard_map/all_gather | solution.py:312
  51.2 139.4 %reduce-scatter.15.cloned.1.call-start = ((), (), s32[]{:S(2)}) async-start(), calls=%async_computation.14 | async-start | bytes 1966080 | tf_op jit(solution)/shard_map/reduce_scatter | solution.py:37
  159.2 31.3 %copy-start.2 = (bf16[1,256,768]{2,1,0:T(8,128)(2,1)S(1)}, bf16[1,256,768]{2,1,0:T(8,128)(2,1)}, u32[]{:S(2)}) copy-start(bf16[1,256,768]{2,1,0:T(8,128)(2,1)} %param.14) | copy-start | bytes 1179652
  164.1 50.8 %all-gather.20.cloned.1.call-start = ((), (), s32[]{:S(2)}) async-start(), calls=%async_computation.15 | async-start | bytes 1966080 | tf_op jit(solution)/shard_map/all_gather | solution.py:33
  164.2 95.4 %copy-start.26 = (f32[768]{0:T(1024)}, f32[768]{0:T(1024)S(1)}, u32[]{:S(2)}) copy-start(f32[768]{0:T(1024)S(1)} %add.276) | copy-start | bytes 9220
  164.3 62.0 %copy-start.28 = (f32[768]{0:T(1024)}, f32[768]{0:T(1024)S(1)}, u32[]{:S(2)}) copy-start(f32[768]{0:T(1024)S(1)} %mul.418) | copy-start | bytes 9220
  191.8 34.5 %copy-start.40 = (f32[256]{0:T(256)}, f32[256]{0:T(256)S(1)}, u32[]{:S(2)}) copy-start(f32[256]{0:T(256)S(1)} %broadcast_multiply_fusion.2) | copy-start | bytes 3076
  193.0 33.2 %copy-start.70 = (f32[256]{0:T(256)}, f32[256]{0:T(256)S(1)}, u32[]{:S(2)}) copy-start(f32[256]{0:T(256)S(1)} %multiply_reduce_fusion.6) | copy-start | bytes 3076
  193.1 33.2 %copy-start.46 = (f32[256]{0:T(256)}, f32[256]{0:T(256)S(1)}, u32[]{:S(2)}) copy-start(f32[256]{0:T(256)S(1)} %fusion.163) | copy-start | bytes 3076
  195.1 64.6 %reduce-scatter.17.cloned.1.call-start = ((), (), s32[]{:S(2)}) async-start(), calls=%async_computation.16 | async-start | bytes 1966080 | tf_op jit(solution)/shard_map/reduce_scatter | solution.py:37
  195.7 30.5 %copy-start.77 = (f32[768]{0:T(1024)}, f32[768]{0:T(1024)S(1)}, u32[]{:S(2)}) copy-start(f32[768]{0:T(1024)S(1)} %add.284) | copy-start | bytes 9220
  231.3 28.4 %copy-start.5 = (bf16[1,256,768]{2,1,0:T(8,128)(2,1)S(1)}, bf16[1,256,768]{2,1,0:T(8,128)(2,1)}, u32[]{:S(2)}) copy-start(bf16[1,256,768]{2,1,0:T(8,128)(2,1)} %reduce-scatter.15.cloned.1.call-done) | copy-start | bytes 1179652
  231.3 108.4 %all-gather.24.cloned.1.call-start = ((), (), s32[]{:S(2)}) async-start(), calls=%async_computation.18 | async-start | bytes 5087232 | tf_op jit(solution)/shard_map/all_gather | solution.py:312
  233.9 125.9 %all-gather.22.cloned.1.call-start = ((), (), s32[]{:S(2)}) async-start(), calls=%async_computation.17 | async-start | bytes 1966080 | tf_op jit(solution)/shard_map/all_gather | solution.py:33
  234.0 28.6 %copy-start.35 = (f32[768]{0:T(1024)}, f32[768]{0:T(1024)S(1)}, u32[]{:S(2)}) copy-start(f32[768]{0:T(1024)S(1)} %mul.427) | copy-start | bytes 9220
  262.2 140.4 %reduce-scatter.19.cloned.1.call-start = ((), (), s32[]{:S(2)}) async-start(), calls=%async_computation.19 | async-start | bytes 1966080 | tf_op jit(solution)/shard_map/reduce_scatter | solution.py:37
  341.6 30.1 %copy-start.14 = (bf16[768,768]{1,0:T(8,128)(2,1)}, bf16[768,768]{1,0:T(8,128)(2,1)S(1)}, u32[]{:S(2)}) copy-start(bf16[768,768]{1,0:T(8,128)(2,1)S(1)} %slice.292) | copy-start | bytes 3538948
  374.2 50.6 %all-gather.26.cloned.1.call-start = ((), (), s32[]{:S(2)}) async-start(), calls=%async_computation.20 | async-start | bytes 1966080 | tf_op jit(solution)/shard_map/all_gather | solution.py:33
  404.9 41.0 %all-gather.28.cloned.1.call-start = ((), (), s32[]{:S(2)}) async-start(), calls=%async_computation.22 | async-start | bytes 1966080 | tf_op jit(solution)/shard_map/all_gather | solution.py:33
  405.5 80.2 %reduce-scatter.23.cloned.1.call-start = ((), (), s32[]{:S(2)}) async-start(), calls=%async_computation.23 | async-start | bytes 1966080 | tf_op jit(solution)/shard_map/reduce_scatter | solution.py:37
  457.4 59.5 %reduce-scatter.21.cloned.1.call-start = ((), (), s32[]{:S(2)}) async-start(), calls=%async_computation.21 | async-start | bytes 1966080 | tf_op jit(solution)/shard_map/reduce_scatter | solution.py:37
  461.7 57.4 %copy-start.11 = (bf16[1,256,768]{2,1,0:T(8,128)(2,1)S(1)}, bf16[1,256,768]{2,1,0:T(8,128)(2,1)}, u32[]{:S(2)}) copy-start(bf16[1,256,768]{2,1,0:T(8,128)(2,1)} %param.27) | copy-start | bytes 1179652
  461.7 78.7 %all-gather.30.cloned.1.call-start = ((), (), s32[]{:S(2)}) async-start(), calls=%async_computation.24 | async-start | bytes 1966080 | tf_op jit(solution)/shard_map/all_gather | solution.py:33
  520.6 82.9 %reduce-scatter.25.cloned.1.call-start = ((), (), s32[]{:S(2)}) async-start(), calls=%async_computation.25 | async-start | bytes 1966080 | tf_op jit(solution)/shard_map/reduce_scatter | solution.py:37
  542.6 13.6 %slice-start.3 = ((s8[12582912]{0:T(1024)(128)(4,1)}), s8[4194304]{0:T(1024)(128)(4,1)S(1)}, s32[]{:S(2)}) async-start(s8[12582912]{0:T(1024)(128)(4,1)} %bitcast.280), calls=%async_computation.38 | async-start | bytes 8388608
  571.3 32.2 %copy-start.36 = (f32[768]{0:T(1024)S(1)}, f32[768]{0:T(1024)}, u32[]{:S(2)}) copy-start(f32[768]{0:T(1024)} %copy-done.35) | copy-start | bytes 9220
  571.4 32.2 %copy-start.45 = (f32[256]{0:T(256)S(1)}, f32[256]{0:T(256)}, u32[]{:S(2)}) copy-start(f32[256]{0:T(256)} %copy-done.44) | copy-start | bytes 3076
  571.4 34.1 %copy-start.73 = (f32[256]{0:T(256)S(1)}, f32[256]{0:T(256)}, u32[]{:S(2)}) copy-start(f32[256]{0:T(256)} %copy-done.72) | copy-start | bytes 3076
  571.4 34.1 %copy-start.65 = (f32[256]{0:T(256)S(1)}, f32[256]{0:T(256)}, u32[]{:S(2)}) copy-start(f32[256]{0:T(256)} %copy-done.64) | copy-start | bytes 3076
  575.2 32.3 %copy-start.75 = (f32[256]{0:T(256)S(1)}, f32[256]{0:T(256)}, u32[]{:S(2)}) copy-start(f32[256]{0:T(256)} %copy-done.74) | copy-start | bytes 3076
  575.2 54.9 %all-gather.32.cloned.1.call-start = ((), (), s32[]{:S(2)}) async-start(), calls=%async_computation.26 | async-start | bytes 1966080 | tf_op jit(solution)/shard_map/all_gather | solution.py:33
  610.3 59.6 %reduce-scatter.27.cloned.1.call-start = ((), (), s32[]{:S(2)}) async-start(), calls=%async_computation.27 | async-start | bytes 1966080 | tf_op jit(solution)/shard_map/reduce_scatter | solution.py:37
  637.7 32.2 %copy-start.27 = (f32[768]{0:T(1024)S(1)}, f32[768]{0:T(1024)}, u32[]{:S(2)}) copy-start(f32[768]{0:T(1024)} %copy-done.26) | copy-start | bytes 9220
  637.7 32.2 %copy-start.29 = (f32[768]{0:T(1024)S(1)}, f32[768]{0:T(1024)}, u32[]{:S(2)}) copy-start(f32[768]{0:T(1024)} %copy-done.28) | copy-start | bytes 9220
  637.7 32.2 %copy-start.41 = (f32[256]{0:T(256)S(1)}, f32[256]{0:T(256)}, u32[]{:S(2)}) copy-start(f32[256]{0:T(256)} %copy-done.40) | copy-start | bytes 3076
  637.7 34.2 %copy-start.71 = (f32[256]{0:T(256)S(1)}, f32[256]{0:T(256)}, u32[]{:S(2)}) copy-start(f32[256]{0:T(256)} %copy-done.70) | copy-start | bytes 3076
  637.7 34.2 %copy-start.47 = (f32[256]{0:T(256)S(1)}, f32[256]{0:T(256)}, u32[]{:S(2)}) copy-start(f32[256]{0:T(256)} %copy-done.46) | copy-start | bytes 3076
  641.6 68.2 %all-gather.34.cloned.1.call-start = ((), (), s32[]{:S(2)}) async-start(), calls=%async_computation.28 | async-start | bytes 1966080 | tf_op jit(solution)/shard_map/all_gather | solution.py:33
  684.3 15.0 %all-to-all-start.1 = ((bf16[192,4,192]{0,2,1:T(8,128)(2,1)}), bf16[192,4,192]{0,2,1:T(8,128)(2,1)S(1)}, u32[]{:S(2)}, u32[]{:S(2)}) async-start(bf16[192,4,192]{0,2,1:T(8,128)(2,1)} %bitcast.61), calls=%async_computation.9 | async-start | bytes 786432 | tf_op jit(solution)/shard_map/all_to_all | solution.py:147
  687.8 100.5 %reduce-scatter.33.cloned.1.call-start = ((), (), s32[]{:S(2)}) async-start(), calls=%async_computation.34 | async-start | bytes 3981312 | tf_op jit(solution)/shard_map/reduce_scatter | solution.py:173
  709.0 110.3 %reduce-scatter.29.cloned.1.call-start = ((), (), s32[]{:S(2)}) async-start(), calls=%async_computation.29 | async-start | bytes 1966080 | tf_op jit(solution)/shard_map/reduce_scatter | solution.py:37
  711.9 8.6 slice-start.2
  747.6 10.9 all-to-all-start
  751.1 150.7 %reduce-scatter.31.cloned.1.call-start = ((), (), s32[]{:S(2)}) async-start(), calls=%async_computation.33 | async-start | bytes 3981312 | tf_op jit(solution)/shard_map/reduce_scatter | solution.py:173
  768.2 20.1 %copy-start.49 = (f32[3,3,64]{2,0,1:T(4,128)S(1)}, f32[3,3,64]{2,0,1:T(4,128)}, u32[]{:S(2)}) copy-start(f32[3,3,64]{2,0,1:T(4,128)} %get-tuple-element.34) | copy-start | bytes 6916
  768.3 51.1 %copy-start.34 = (f32[768]{0:T(1024)S(1)}, f32[768]{0:T(1024)}, u32[]{:S(2)}) copy-start(f32[768]{0:T(1024)} %copy-done.33) | copy-start | bytes 9220
  768.3 51.1 %copy-start.43 = (f32[256]{0:T(256)S(1)}, f32[256]{0:T(256)}, u32[]{:S(2)}) copy-start(f32[256]{0:T(256)} %copy-done.42) | copy-start | bytes 3076
  768.3 52.4 %copy-start.69 = (f32[256]{0:T(256)S(1)}, f32[256]{0:T(256)}, u32[]{:S(2)}) copy-start(f32[256]{0:T(256)} %copy-done.68) | copy-start | bytes 3076
  768.3 52.4 %copy-start.53 = (f32[256]{0:T(256)S(1)}, f32[256]{0:T(256)}, u32[]{:S(2)}) copy-start(f32[256]{0:T(256)} %copy-done.52) | copy-start | bytes 3076
  768.3 54.0 %copy-start.59 = (f32[768]{0:T(1024)S(1)}, f32[768]{0:T(1024)}, u32[]{:S(2)}) copy-start(f32[768]{0:T(1024)} %get-tuple-element.32) | copy-start | bytes 9220
  768.3 54.0 %copy-start.58 = (f32[768]{0:T(1024)S(1)}, f32[768]{0:T(1024)}, u32[]{:S(2)}) copy-start(f32[768]{0:T(1024)} %get-tuple-element.14) | copy-start | bytes 9220
  768.3 54.0 %copy-start.57 = (f32[768]{0:T(1024)S(1)}, f32[768]{0:T(1024)}, u32[]{:S(2)}) copy-start(f32[768]{0:T(1024)} %get-tuple-element.22) | copy-start | bytes 9220
  768.3 54.0 %copy-start.62 = (f32[768]{0:T(1024)S(1)}, f32[768]{0:T(1024)}, u32[]{:S(2)}) copy-start(f32[768]{0:T(1024)} %get-tuple-element.29) | copy-start | bytes 9220
  768.4 155.3 %all-gather.38.cloned.1.call-start = ((), (), s32[]{:S(2)}) async-start(), calls=%async_computation.32 | async-start | bytes 2211840 | tf_op jit(solution)/shard_map/all_gather | solution.py:174
  788.3 259.3 %all-reduce.2.cloned.1.call-start = ((), (), s32[]{:S(2)}) async-start(), calls=%async_computation.30 | async-start | bytes 147456 | tf_op jit(solution)/shard_map/psum | solution.py:358
  823.1 248.8 %all-gather.36.cloned.1.call-start = ((), (), s32[]{:S(2)}) async-start(), calls=%async_computation.31 | async-start | bytes 2211840 | tf_op jit(solution)/shard_map/all_gather | solution.py:174
  928.3 8.8 copy-start.6
  928.3 8.8 copy-start.10
  928.3 8.8 copy-start.51
  928.3 8.8 copy-start.67
  (53 other events, 151.4 us)
Sparse Core Ops, SparseCore 0:
  46.5 20.5 all-gather.15
  69.8 77.4 all-gather.17
  164.2 26.3 reduce-scatter.14
  195.2 19.6 all-gather.19
  231.4 28.1 reduce-scatter.16
  262.2 77.4 all-gather.23
  341.9 17.8 all-gather.21
  374.3 28.1 reduce-scatter.18
  405.0 19.6 all-gather.25
  426.2 19.6 all-gather.27
  457.5 28.1 reduce-scatter.22
  488.7 28.1 reduce-scatter.20
  520.8 19.6 all-gather.29
  575.4 28.1 reduce-scatter.24
  610.4 19.6 all-gather.31
  641.8 28.1 reduce-scatter.26
  677.0 23.7 all-gather.33
  709.2 79.0 reduce-scatter.32
  791.6 27.7 reduce-scatter.28
  822.8 78.9 reduce-scatter.30
  903.4 20.2 all-gather.37
  929.3 118.3 all-reduce.1
  1049.2 22.6 all-gather.35
where the time goes:
time: 1100 us; the launch traced here: 1090 us
  waiting for transfers between devices  753 us (68%)
  matrix products  139 us (13%)
  local copies, waits for them, and re-layouts  74.5 us (7%)
  other arithmetic  69.5 us (6%)
  blocking collectives  32.3 us (3%)
  between operations  15.9 us (1%)
    reduce_scatter x8, waiting for transfers between devices, seq_reduce(): lax.psum_scatter(partial_sum.astype(BF), 'seq', scatter_dimension=1, tile...  219 us
    all_gather x2, waiting for transfers between devices, local(): packed = lax.all_gather(packed, 'fsdp', axis=0, tiled=True)  157 us
    all_gather x8, waiting for transfers between devices, seq_gather(): return lax.all_gather(block, 'seq', axis=1, tiled=True)  119 us
    psum x1, waiting for transfers between devices, local(): small_sum = lax.psum(jnp.stack(smalls), ('seq', 'fsdp'))  109 us
    reduce_scatter x2, waiting for transfers between devices, reduce_big(): owned = lax.psum_scatter(big, 'fsdp', scatter_dimension=0, tiled=True)  96.8 us
    dot_general x8, matrix products, dot_in(): return jnp.einsum('cfi,io->cfo', rows, matrix, preferred_element_type=F32)  40.2 us
    all_gather x2, waiting for transfers between devices, reduce_big(): return lax.all_gather(owned, 'seq', axis=0, tiled=False)  39.4 us
    dot_general x8, matrix products, dot_back(): return jnp.einsum('cfo,io->cfi', rows, matrix, preferred_element_type=F32)  32.4 us
  transfers between devices with their start and end apart: 25, of which 24 were waited for; matrix products, arithmetic and copies ran while one was open for 12% of the time, Pallas kernels for 0%

commit v1 on v0

--- a/solution.py
+++ b/solution.py
@@ -309,7 +309,26 @@
             ],
             axis=1,
         )
-        packed = lax.all_gather(packed, "fsdp", axis=0, tiled=True)
+        size_2, index_2, rows_2 = (lax.axis_size("fsdp"), lax.axis_index("fsdp"), packed.shape[0])
+        upward = [(i_2, (i_2 + 1) % size_2) for i_2 in range(size_2)]
+        left_2 = [(i_2, (i_2 - 1) % size_2) for i_2 in range(size_2)]
+        out_2 = jnp.zeros(
+            (*packed.shape[:0], size_2 * rows_2, *packed.shape[0 + 1 :]), packed.dtype
+        )
+        out_2 = lax.dynamic_update_slice_in_dim(out_2, packed, index_2 * rows_2, axis=0)
+        from_left = from_right = packed
+        middle = size_2 // 2
+        for turn in range(1, middle + 1):
+            from_left = lax.ppermute(from_left, "fsdp", upward)
+            out_2 = lax.dynamic_update_slice_in_dim(
+                out_2, from_left, (index_2 - turn) % size_2 * rows_2, axis=0
+            )
+            if turn < size_2 - middle:
+                from_right = lax.ppermute(from_right, "fsdp", left_2)
+                out_2 = lax.dynamic_update_slice_in_dim(
+                    out_2, from_right, (index_2 + turn) % size_2 * rows_2, axis=0
+                )
+        packed = out_2
         third = 3 * D // seq_size
         w_up = packed[:, :hidden_local]
         w_down = packed[:, hidden_local : hidden_local + D]

time: 1100 us -> 1060 us (0.964)
  waiting for transfers between devices: 753 us -> 661 us
  starting transfers between devices: 9.47 us -> 35.8 us
  blocking collectives: 32.3 us -> 45.1 us
  local copies, waits for them, and re-layouts: 74.5 us -> 87.2 us
    all_gather x2 -> x0, waiting for transfers between devices: 157 us -> none  [local(): packed = lax.all_gather(packed, 'fsdp', axis=0, tiled=True)]
    ppermute x0 -> x14, waiting for transfers between devices: none -> 127 us  [the longest x8 65.3 us: local(): from_left = lax.ppermute(from_left, 'fsdp', upward)]
    all_gather x8, waiting for transfers between devices: 119 us -> 86.2 us  [seq_gather(): return lax.all_gather(block, 'seq', axis=1, tiled=True)]
    reduce_scatter x8, waiting for transfers between devices: 219 us -> 191 us  [seq_reduce(): lax.psum_scatter(partial_sum.astype(BF), 'seq', scatter_dimension=1, tile...]
    ppermute x0 -> x14, starting transfers between devices: none -> 26.8 us  [the longest x6 19.5 us: local(): from_right = lax.ppermute(from_right, 'fsdp', left_2)]
    all_gather x1, blocking collectives: 32.3 us -> 45.1 us  [local(): lax.all_gather(small_in.reshape(-1), 'fsdp', axis=0, tiled=False)]
    unnamed x207 -> x239, local copies, waits for them, and re-layouts: 27.4 us -> 29.1 us
  transfers between devices with their start and end apart: 25 -> 37, of which waited for: 24 -> 27; matrix products, arithmetic and copies ran while one was open for 12% -> 13% of each run, Pallas kernels for 0% -> 0%
where the time goes in v1:
time: 1060 us; the launch traced here: 1050 us
  waiting for transfers between devices  661 us (62%)
  matrix products  140 us (13%)
  local copies, waits for them, and re-layouts  87.2 us (8%)
  other arithmetic  66.4 us (6%)
  blocking collectives  45.1 us (4%)
  starting transfers between devices  35.8 us (3%)
  between operations  16.7 us (2%)
    reduce_scatter x8, waiting for transfers between devices, seq_reduce(): lax.psum_scatter(partial_sum.astype(BF), 'seq', scatter_dimension=1, tile...  191 us
    psum x1, waiting for transfers between devices, local(): small_sum = lax.psum(jnp.stack(smalls), ('seq', 'fsdp'))  109 us
    reduce_scatter x2, waiting for transfers between devices, reduce_big(): owned = lax.psum_scatter(big, 'fsdp', scatter_dimension=0, tiled=True)  96.5 us
    all_gather x8, waiting for transfers between devices, seq_gather(): return lax.all_gather(block, 'seq', axis=1, tiled=True)  86.2 us
    ppermute x8, waiting for transfers between devices, local(): from_left = lax.ppermute(from_left, 'fsdp', upward)  65.3 us
    ppermute x6, waiting for transfers between devices, local(): from_right = lax.ppermute(from_right, 'fsdp', left_2)  61.3 us
    all_gather x1, blocking collectives, local(): lax.all_gather(small_in.reshape(-1), 'fsdp', axis=0, tiled=False)  45.1 us
    dot_general x8, matrix products, dot_in(): return jnp.einsum('cfi,io->cfo', rows, matrix, preferred_element_type=F32)  41.6 us
  transfers between devices with their start and end apart: 37, of which 27 were waited for; matrix products, arithmetic and copies ran while one was open for 13% of the time, Pallas kernels for 0%

profile of v1, /device:TPU:0, one launch (start us, length us, event | category | flops | bytes accessed | tf_op | source)
XLA Modules:
  0.0 1052.3 jit_solution(2112820597044167185)
XLA Ops:
  14.1 6.0 collective-permute-start.1
  21.3 45.1 %all-gather.2 = bf16[8,1,2304]{2,1,0:T(2,128)(2,1)S(1)} all-gather(bf16[1,1,2304]{2,1,0:T(2,128)(2,1)S(1)} %reshape.700), channel_id=1, replica_groups=mesh['seq'=4,'fsdp'=8] {'fsdp'}, dimensions={0}, use_global_device_ids=true | all-gather | bytes 41472 | tf_op jit(solution)/shard_map/all_gather | solution.py:298
  69.9 4.5 collective-permute-start.3
  74.6 22.3 %collective-permute-done.3 = bf16[96,2880]{1,0:T(8,128)(2,1)S(1)} collective-permute-done((bf16[96,2880]{1,0:T(8,128)(2,1)S(1)}, bf16[96,2880]{1,0:T(8,128)(2,1)S(1)}, u32[]{:S(2)}, u32[]{:S(2)}) %collective-permute-start.3) | collective-permute-done | bytes 552992 | tf_op jit(solution)/shard_map/ppermute | solution.py:327
  99.1 16.5 %collective-permute-done.4 = bf16[96,2880]{1,0:T(8,128)(2,1)S(1)} collective-permute-done((bf16[96,2880]{1,0:T(8,128)(2,1)S(1)}, bf16[96,2880]{1,0:T(8,128)(2,1)S(1)}, u32[]{:S(2)}, u32[]{:S(2)}) %collective-permute-start.4) | collective-permute-done | bytes 552992 | tf_op jit(solution)/shard_map/ppermute | solution.py:322
  118.4 14.2 %collective-permute-done.6 = bf16[96,2880]{1,0:T(8,128)(2,1)S(1)} collective-permute-done((bf16[96,2880]{1,0:T(8,128)(2,1)S(1)}, bf16[96,2880]{1,0:T(8,128)(2,1)S(1)}, u32[]{:S(2)}, u32[]{:S(2)}) %collective-permute-start.6) | collective-permute-done | bytes 552992 | tf_op jit(solution)/shard_map/ppermute | solution.py:322
  135.4 3.2 add_convert_fusion.2
  145.1 2.6 fusion.103
  150.8 26.5 %reduce-scatter.15.cloned.1.call-done = bf16[1,256,768]{2,1,0:T(8,128)(2,1)} async-done(((bf16[1,1024,768]{2,1,0:T(8,128)(2,1)}), bf16[1,256,768]{2,1,0:T(8,128)(2,1)}) %reduce-scatter.15.cloned.1.call-update) | async-done | bytes 393232 | tf_op jit(solution)/shard_map/reduce_scatter | solution.py:37
  182.0 19.6 %all-gather.16.cloned.1.call-done = bf16[1,1024,768]{2,1,0:T(8,128)(2,1)} async-done(((bf16[1,256,768]{2,1,0:T(8,128)(2,1)}), bf16[1,1024,768]{2,1,0:T(8,128)(2,1)}) %all-gather.16.cloned.1.call-update) | async-done | bytes 1572880 | tf_op jit(solution)/shard_map/all_gather | solution.py:33
  201.6 11.4 %multiply_convert_fusion.3 = (bf16[1024,768]{1,0:T(8,128)(2,1)S(1)}, f32[1024,768]{1,0:T(8,128)}, f32[1024,768]{1,0:T(8,128)}) fusion(f32[768]{0:T(1024)S(1)} %add.377, bf16[768,2880]{1,0:T(8,128)(2,1)} %copy-done.6, bf16[1,1024,768]{2,1,0:T(8,128)(2,1)} %all-gather.16.cloned.1.call-done), kind=kOutput, calls=%fused_computation.51 | convolution fusion | flops 1259864064 | bytes 10619904 | tf_op jit(solution)/shard_map/cfi,io->cfo/dot_general | solution.py:42
  213.0 4.4 fusion.73
  220.2 4.3 collective-permute-start.8
  228.1 19.2 %collective-permute-done.8 = bf16[96,2880]{1,0:T(8,128)(2,1)S(1)} collective-permute-done((bf16[96,2880]{1,0:T(8,128)(2,1)S(1)}, bf16[96,2880]{1,0:T(8,128)(2,1)S(1)}, u32[]{:S(2)}, u32[]{:S(2)}) %collective-permute-start.8) | collective-permute-done | bytes 552992 | tf_op jit(solution)/shard_map/ppermute | solution.py:327
  254.0 19.5 %collective-permute-done.10 = bf16[96,2880]{1,0:T(8,128)(2,1)S(1)} collective-permute-done((bf16[96,2880]{1,0:T(8,128)(2,1)S(1)}, bf16[96,2880]{1,0:T(8,128)(2,1)S(1)}, u32[]{:S(2)}, u32[]{:S(2)}) %collective-permute-start.10) | collective-permute-done | bytes 552992 | tf_op jit(solution)/shard_map/ppermute | solution.py:327
  278.7 19.2 %collective-permute-done.11 = bf16[96,2880]{1,0:T(8,128)(2,1)S(1)} collective-permute-done((bf16[96,2880]{1,0:T(8,128)(2,1)}, bf16[96,2880]{1,0:T(8,128)(2,1)S(1)}, u32[]{:S(2)}, u32[]{:S(2)}) %collective-permute-start.11) | collective-permute-done | bytes 552992 | tf_op jit(solution)/shard_map/ppermute | solution.py:322
  297.9 2.8 collective-permute-start.13
  302.4 15.4 %collective-permute-done.13 = bf16[96,2880]{1,0:T(8,128)(2,1)S(1)} collective-permute-done((bf16[96,2880]{1,0:T(8,128)(2,1)S(1)}, bf16[96,2880]{1,0:T(8,128)(2,1)S(1)}, u32[]{:S(2)}, u32[]{:S(2)}) %collective-permute-start.13) | collective-permute-done | bytes 552992 | tf_op jit(solution)/shard_map/ppermute | solution.py:322
  320.5 3.2 add_convert_fusion.1
  330.2 2.6 fusion.102
  335.7 25.6 %reduce-scatter.19.cloned.1.call-done = bf16[1,256,768]{2,1,0:T(8,128)(2,1)} async-done(((bf16[1,1024,768]{2,1,0:T(8,128)(2,1)}), bf16[1,256,768]{2,1,0:T(8,128)(2,1)}) %reduce-scatter.19.cloned.1.call-update) | async-done | bytes 393232 | tf_op jit(solution)/shard_map/reduce_scatter | solution.py:37
  364.8 18.7 %all-gather.20.cloned.1.call-done = bf16[1,1024,768]{2,1,0:T(8,128)(2,1)} async-done(((bf16[1,256,768]{2,1,0:T(8,128)(2,1)}), bf16[1,1024,768]{2,1,0:T(8,128)(2,1)}) %all-gather.20.cloned.1.call-update) | async-done | bytes 1572880 | tf_op jit(solution)/shard_map/all_gather | solution.py:33
  383.5 11.6 %multiply_convert_fusion.2 = (bf16[1024,768]{1,0:T(8,128)(2,1)}, f32[1024,768]{1,0:T(8,128)}, f32[1024,768]{1,0:T(8,128)}) fusion(f32[768]{0:T(1024)S(1)} %add.398, bf16[768,2880]{1,0:T(8,128)(2,1)} %constant_dynamic-update-slice_fusion, bf16[1,1024,768]{2,1,0:T(8,128)(2,1)} %all-gather.20.cloned.1.call-done), kind=kOutput, calls=%fused_computation.38 | convolution fusion | flops 1259864064 | bytes 10619904 | tf_op jit(solution)/shard_map/cfi,io->cfo/dot_general | solution.py:42
  395.1 9.7 all-gather.22.cloned.1.call-done
  404.9 6.4 convert_reduce_fusion
  412.5 3.8 fusion.76
  416.4 4.3 fusion.75
  420.8 23.9 %reduce-scatter.23.cloned.1.call-done = bf16[1,256,768]{2,1,0:T(8,128)(2,1)} async-done(((bf16[1,1024,768]{2,1,0:T(8,128)(2,1)}), bf16[1,256,768]{2,1,0:T(8,128)(2,1)}) %reduce-scatter.23.cloned.1.call-update) | async-done | bytes 393232 | tf_op jit(solution)/shard_map/reduce_scatter | solution.py:37
  447.2 28.7 %reduce-scatter.21.cloned.1.call-done = bf16[1,256,768]{2,1,0:T(8,128)(2,1)} async-done(((bf16[1,1024,768]{2,1,0:T(8,128)(2,1)}), bf16[1,256,768]{2,1,0:T(8,128)(2,1)}) %reduce-scatter.21.cloned.1.call-update) | async-done | bytes 393232 | tf_op jit(solution)/shard_map/reduce_scatter | solution.py:37
  480.6 18.8 %all-gather.24.cloned.1.call-done = bf16[1,1024,768]{2,1,0:T(8,128)(2,1)} async-done(((bf16[1,256,768]{2,1,0:T(8,128)(2,1)}), bf16[1,1024,768]{2,1,0:T(8,128)(2,1)}) %all-gather.24.cloned.1.call-update) | async-done | bytes 1572880 | tf_op jit(solution)/shard_map/all_gather | solution.py:33
  501.5 7.0 fusion.93
  508.6 6.6 multiply_reduce_fusion.1
  515.7 5.3 multiply_convert_fusion.1
  521.0 5.1 fusion.88
  530.3 3.9 fusion.78
  534.2 28.2 %reduce-scatter.25.cloned.1.call-done = bf16[1,256,768]{2,1,0:T(8,128)(2,1)} async-done(((bf16[1,1024,768]{2,1,0:T(8,128)(2,1)}), bf16[1,256,768]{2,1,0:T(8,128)(2,1)}) %reduce-scatter.25.cloned.1.call-update) | async-done | bytes 393232 | tf_op jit(solution)/shard_map/reduce_scatter | solution.py:37
  566.4 2.8 convert_reduce_fusion.11
  569.7 19.4 %all-gather.26.cloned.1.call-done = bf16[1,1024,768]{2,1,0:T(8,128)(2,1)} async-done(((bf16[1,256,768]{2,1,0:T(8,128)(2,1)}), bf16[1,1024,768]{2,1,0:T(8,128)(2,1)}) %all-gather.26.cloned.1.call-update) | async-done | bytes 1572880 | tf_op jit(solution)/shard_map/all_gather | solution.py:33
  589.0 6.4 convert_reduce_fusion.1
  596.6 3.9 fusion.77
  600.6 28.3 %reduce-scatter.27.cloned.1.call-done = bf16[1,256,768]{2,1,0:T(8,128)(2,1)} async-done(((bf16[1,1024,768]{2,1,0:T(8,128)(2,1)}), bf16[1,256,768]{2,1,0:T(8,128)(2,1)}) %reduce-scatter.27.cloned.1.call-update) | async-done | bytes 393232 | tf_op jit(solution)/shard_map/reduce_scatter | solution.py:37
  633.0 2.7 convert_reduce_fusion.12
  635.8 3.5 fusion.66
  643.2 3.5 all-to-all-start.1
  646.7 3.8 fusion.83
  650.5 7.8 all-to-all-done.1
  658.9 3.2 pad_maximum_fusion.1
  662.1 5.8 copy.193
  670.9 6.9 multiply_reduce_fusion
  679.4 5.3 multiply_convert_fusion
  684.7 5.0 fusion.86
  695.2 3.8 fusion.79
  699.1 3.5 fusion.69
  706.6 3.5 all-to-all-start
  710.3 3.8 fusion.80
  714.1 3.3 all-to-all-done
  718.1 3.3 pad_maximum_fusion
  721.4 5.8 copy.191
  729.2 17.8 %reduce-scatter.33.cloned.1.call-done = bf16[96,2304]{1,0:T(8,128)(2,1)} async-done(((bf16[768,2304]{1,0:T(8,128)(2,1)}), bf16[96,2304]{1,0:T(8,128)(2,1)}) %reduce-scatter.33.cloned.1.call-update) | async-done | bytes 442384 | tf_op jit(solution)/shard_map/reduce_scatter | solution.py:173
  747.6 30.3 %reduce-scatter.29.cloned.1.call-done = bf16[1,256,768]{2,1,0:T(8,128)(2,1)} async-done(((bf16[1,1024,768]{2,1,0:T(8,128)(2,1)}), bf16[1,256,768]{2,1,0:T(8,128)(2,1)}) %reduce-scatter.29.cloned.1.call-update) | async-done | bytes 393232 | tf_op jit(solution)/shard_map/reduce_scatter | solution.py:37
  781.7 78.7 %reduce-scatter.31.cloned.1.call-done = bf16[96,2304]{1,0:T(8,128)(2,1)} async-done(((bf16[768,2304]{1,0:T(8,128)(2,1)}), bf16[96,2304]{1,0:T(8,128)(2,1)}) %reduce-scatter.31.cloned.1.call-update) | async-done | bytes 442384 | tf_op jit(solution)/shard_map/reduce_scatter | solution.py:173
  860.4 21.9 %all-gather.32.cloned.1.call-done = bf16[384,2304]{1,0:T(8,128)(2,1)} async-done(((bf16[96,2304]{1,0:T(8,128)(2,1)}), bf16[384,2304]{1,0:T(8,128)(2,1)}) %all-gather.32.cloned.1.call-update) | async-done | bytes 1769488 | tf_op jit(solution)/shard_map/all_gather | solution.py:174
  897.3 108.8 %all-reduce.2.cloned.1.call-done = f32[2,9216]{1,0:T(2,128)} async-done(((f32[2,9216]{1,0:T(2,128)}), f32[2,9216]{1,0:T(2,128)}) %all-reduce.2.cloned.1.call-update) | async-done | bytes 73744 | tf_op jit(solution)/shard_map/psum | solution.py:377
  1012.8 17.6 %all-gather.30.cloned.1.call-done = bf16[384,2304]{1,0:T(8,128)(2,1)} async-done(((bf16[96,2304]{1,0:T(8,128)(2,1)}), bf16[384,2304]{1,0:T(8,128)(2,1)}) %all-gather.30.cloned.1.call-update) | async-done | bytes 1769488 | tf_op jit(solution)/shard_map/all_gather | solution.py:174
  (502 shorter events, 155.2 us)
Async XLA Ops:
  7.2 128.2 %all-gather.14.cloned.1.call-start = ((), (), s32[]{:S(2)}) async-start(), calls=%async_computation.12 | async-start | bytes 1966080 | tf_op jit(solution)/shard_map/all_gather | solution.py:33
  14.1 55.8 %collective-permute-start.1 = (bf16[96,2880]{1,0:T(8,128)(2,1)S(1)}, bf16[96,2880]{1,0:T(8,128)(2,1)S(1)}, u32[]{:S(2)}, u32[]{:S(2)}) collective-permute-start(bf16[96,2880]{1,0:T(8,128)(2,1)S(1)} %concatenate.28), channel_id=1, source_target_pairs={{0,7},{1,0},{2,1},{3,2},{4,3},{5,4},{6,5},{7,6},{8,15},{9,8},{10,9... | collective-permute-start | bytes 1658888 | tf_op jit(solution)/shard_map/ppermute | solution.py:327
  20.1 54.3 %collective-permute-start = (bf16[96,2880]{1,0:T(8,128)(2,1)S(1)}, bf16[96,2880]{1,0:T(8,128)(2,1)S(1)}, u32[]{:S(2)}, u32[]{:S(2)}) collective-permute-start(bf16[96,2880]{1,0:T(8,128)(2,1)S(1)} %concatenate.28), channel_id=1, source_target_pairs={{0,1},{1,2},{2,3},{3,4},{4,5},{5,6},{6,7},{7,0},{8,9},{9,10},{10,1... | collective-permute-start | bytes 1658888 | tf_op jit(solution)/shard_map/ppermute | solution.py:322
  20.3 49.0 %copy-start.44 = (f32[256]{0:T(256)}, f32[256]{0:T(256)S(1)}, u32[]{:S(2)}) copy-start(f32[256]{0:T(256)S(1)} %broadcast_multiply_fusion.3) | copy-start | bytes 3076
  20.6 48.5 %copy-start.54 = (f32[256]{0:T(256)}, f32[256]{0:T(256)S(1)}, u32[]{:S(2)}) copy-start(f32[256]{0:T(256)S(1)} %fusion.162) | copy-start | bytes 3076
  68.0 109.2 %reduce-scatter.15.cloned.1.call-start = ((), (), s32[]{:S(2)}) async-start(), calls=%async_computation.13 | async-start | bytes 1966080 | tf_op jit(solution)/shard_map/reduce_scatter | solution.py:37
  69.9 27.0 %collective-permute-start.3 = (bf16[96,2880]{1,0:T(8,128)(2,1)S(1)}, bf16[96,2880]{1,0:T(8,128)(2,1)S(1)}, u32[]{:S(2)}, u32[]{:S(2)}) collective-permute-start(bf16[96,2880]{1,0:T(8,128)(2,1)S(1)} %collective-permute-done.1), channel_id=1, source_target_pairs={{0,7},{1,0},{2,1},{3,2},{4,3},{5,4},{6,5},{7,6},{8,15},{9,8},{10,9... | collective-permute-start | bytes 1658888 | tf_op jit(solution)/shard_map/ppermute | solution.py:327
  74.5 22.5 %collective-permute-start.2 = (bf16[96,2880]{1,0:T(8,128)(2,1)S(1)}, bf16[96,2880]{1,0:T(8,128)(2,1)S(1)}, u32[]{:S(2)}, u32[]{:S(2)}) collective-permute-start(bf16[96,2880]{1,0:T(8,128)(2,1)S(1)} %collective-permute-done), channel_id=1, source_target_pairs={{0,1},{1,2},{2,3},{3,4},{4,5},{5,6},{6,7},{7,0},{8,9},{9,10},{10,1... | collective-permute-start | bytes 1658888 | tf_op jit(solution)/shard_map/ppermute | solution.py:322
  96.9 21.4 %collective-permute-start.5 = (bf16[96,2880]{1,0:T(8,128)(2,1)S(1)}, bf16[96,2880]{1,0:T(8,128)(2,1)S(1)}, u32[]{:S(2)}, u32[]{:S(2)}) collective-permute-start(bf16[96,2880]{1,0:T(8,128)(2,1)S(1)} %collective-permute-done.3), channel_id=1, source_target_pairs={{0,7},{1,0},{2,1},{3,2},{4,3},{5,4},{6,5},{7,6},{8,15},{9,8},{10,9... | collective-permute-start | bytes 1658888 | tf_op jit(solution)/shard_map/ppermute | solution.py:327
  96.9 18.7 %collective-permute-start.4 = (bf16[96,2880]{1,0:T(8,128)(2,1)S(1)}, bf16[96,2880]{1,0:T(8,128)(2,1)S(1)}, u32[]{:S(2)}, u32[]{:S(2)}) collective-permute-start(bf16[96,2880]{1,0:T(8,128)(2,1)S(1)} %collective-permute-done.2), channel_id=1, source_target_pairs={{0,1},{1,2},{2,3},{3,4},{4,5},{5,6},{6,7},{7,0},{8,9},{9,10},{10,1... | collective-permute-start | bytes 1658888 | tf_op jit(solution)/shard_map/ppermute | solution.py:322
  115.6 17.0 %collective-permute-start.6 = (bf16[96,2880]{1,0:T(8,128)(2,1)S(1)}, bf16[96,2880]{1,0:T(8,128)(2,1)S(1)}, u32[]{:S(2)}, u32[]{:S(2)}) collective-permute-start(bf16[96,2880]{1,0:T(8,128)(2,1)S(1)} %collective-permute-done.4), channel_id=1, source_target_pairs={{0,1},{1,2},{2,3},{3,4},{4,5},{5,6},{6,7},{7,0},{8,9},{9,10},{10,1... | collective-permute-start | bytes 1658888 | tf_op jit(solution)/shard_map/ppermute | solution.py:322
  150.3 51.3 %all-gather.16.cloned.1.call-start = ((), (), s32[]{:S(2)}) async-start(), calls=%async_computation.14 | async-start | bytes 1966080 | tf_op jit(solution)/shard_map/all_gather | solution.py:33
  150.6 99.0 %copy-start.28 = (f32[768]{0:T(1024)}, f32[768]{0:T(1024)S(1)}, u32[]{:S(2)}) copy-start(f32[768]{0:T(1024)S(1)} %add.369) | copy-start | bytes 9220
  150.7 62.3 %copy-start.30 = (f32[768]{0:T(1024)}, f32[768]{0:T(1024)S(1)}, u32[]{:S(2)}) copy-start(f32[768]{0:T(1024)S(1)} %mul.456) | copy-start | bytes 9220
  178.5 34.5 %copy-start.42 = (f32[256]{0:T(256)}, f32[256]{0:T(256)S(1)}, u32[]{:S(2)}) copy-start(f32[256]{0:T(256)S(1)} %broadcast_multiply_fusion.2) | copy-start | bytes 3076
  179.8 33.2 %copy-start.48 = (f32[256]{0:T(256)}, f32[256]{0:T(256)S(1)}, u32[]{:S(2)}) copy-start(f32[256]{0:T(256)S(1)} %fusion.163) | copy-start | bytes 3076
  181.8 67.9 %reduce-scatter.17.cloned.1.call-start = ((), (), s32[]{:S(2)}) async-start(), calls=%async_computation.15 | async-start | bytes 1966080 | tf_op jit(solution)/shard_map/reduce_scatter | solution.py:37
  217.4 103.1 %all-gather.18.cloned.1.call-start = ((), (), s32[]{:S(2)}) async-start(), calls=%async_computation.16 | async-start | bytes 1966080 | tf_op jit(solution)/shard_map/all_gather | solution.py:33
  220.2 27.1 %collective-permute-start.8 = (bf16[96,2880]{1,0:T(8,128)(2,1)S(1)}, bf16[96,2880]{1,0:T(8,128)(2,1)S(1)}, u32[]{:S(2)}, u32[]{:S(2)}) collective-permute-start(bf16[96,2880]{1,0:T(8,128)(2,1)S(1)} %concatenate.30), channel_id=1, source_target_pairs={{0,7},{1,0},{2,1},{3,2},{4,3},{5,4},{6,5},{7,6},{8,15},{9,8},{10,9... | collective-permute-start | bytes 1658888 | tf_op jit(solution)/shard_map/ppermute | solution.py:327
  224.5 25.1 %collective-permute-start.7 = (bf16[96,2880]{1,0:T(8,128)(2,1)S(1)}, bf16[96,2880]{1,0:T(8,128)(2,1)S(1)}, u32[]{:S(2)}, u32[]{:S(2)}) collective-permute-start(bf16[96,2880]{1,0:T(8,128)(2,1)S(1)} %concatenate.30), channel_id=1, source_target_pairs={{0,1},{1,2},{2,3},{3,4},{4,5},{5,6},{6,7},{7,0},{8,9},{9,10},{10,1... | collective-permute-start | bytes 1658888 | tf_op jit(solution)/shard_map/ppermute | solution.py:322
  247.3 26.2 %collective-permute-start.10 = (bf16[96,2880]{1,0:T(8,128)(2,1)S(1)}, bf16[96,2880]{1,0:T(8,128)(2,1)S(1)}, u32[]{:S(2)}, u32[]{:S(2)}) collective-permute-start(bf16[96,2880]{1,0:T(8,128)(2,1)S(1)} %collective-permute-done.8), channel_id=1, source_target_pairs={{0,7},{1,0},{2,1},{3,2},{4,3},{5,4},{6,5},{7,6},{8,15},{9,8},{10,9... | collective-permute-start | bytes 1658888 | tf_op jit(solution)/shard_map/ppermute | solution.py:327
  249.6 26.2 %collective-permute-start.9 = (bf16[96,2880]{1,0:T(8,128)(2,1)S(1)}, bf16[96,2880]{1,0:T(8,128)(2,1)}, u32[]{:S(2)}, u32[]{:S(2)}) collective-permute-start(bf16[96,2880]{1,0:T(8,128)(2,1)S(1)} %collective-permute-done.7), channel_id=1, source_target_pairs={{0,1},{1,2},{2,3},{3,4},{4,5},{5,6},{6,7},{7,0},{8,9},{9,10},{10,1... | collective-permute-start | bytes 1658888 | tf_op jit(solution)/shard_map/ppermute | solution.py:322
  251.2 50.3 %copy-start.80 = (f32[256]{0:T(256)}, f32[256]{0:T(256)S(1)}, u32[]{:S(2)}) copy-start(f32[256]{0:T(256)S(1)} %multiply_reduce_fusion.5) | copy-start | bytes 3076
  251.2 50.3 %copy-start.72 = (f32[256]{0:T(256)}, f32[256]{0:T(256)S(1)}, u32[]{:S(2)}) copy-start(f32[256]{0:T(256)S(1)} %fusion.164) | copy-start | bytes 3076
  252.2 109.1 %reduce-scatter.19.cloned.1.call-start = ((), (), s32[]{:S(2)}) async-start(), calls=%async_computation.17 | async-start | bytes 1966080 | tf_op jit(solution)/shard_map/reduce_scatter | solution.py:37
  273.5 28.0 %collective-permute-start.12 = (bf16[96,2880]{1,0:T(8,128)(2,1)S(1)}, bf16[96,2880]{1,0:T(8,128)(2,1)S(1)}, u32[]{:S(2)}, u32[]{:S(2)}) collective-permute-start(bf16[96,2880]{1,0:T(8,128)(2,1)S(1)} %collective-permute-done.10), channel_id=1, source_target_pairs={{0,7},{1,0},{2,1},{3,2},{4,3},{5,4},{6,5},{7,6},{8,15},{9,8},{10,9... | collective-permute-start | bytes 1658888 | tf_op jit(solution)/shard_map/ppermute | solution.py:327
  275.9 22.0 %collective-permute-start.11 = (bf16[96,2880]{1,0:T(8,128)(2,1)}, bf16[96,2880]{1,0:T(8,128)(2,1)S(1)}, u32[]{:S(2)}, u32[]{:S(2)}) collective-permute-start(bf16[96,2880]{1,0:T(8,128)(2,1)} %collective-permute-done.9), channel_id=1, source_target_pairs={{0,1},{1,2},{2,3},{3,4},{4,5},{5,6},{6,7},{7,0},{8,9},{9,10},{10,1... | collective-permute-start | bytes 1658888 | tf_op jit(solution)/shard_map/ppermute | solution.py:322
  297.9 19.9 %collective-permute-start.13 = (bf16[96,2880]{1,0:T(8,128)(2,1)S(1)}, bf16[96,2880]{1,0:T(8,128)(2,1)S(1)}, u32[]{:S(2)}, u32[]{:S(2)}) collective-permute-start(bf16[96,2880]{1,0:T(8,128)(2,1)S(1)} %collective-permute-done.11), channel_id=1, source_target_pairs={{0,1},{1,2},{2,3},{3,4},{4,5},{5,6},{6,7},{7,0},{8,9},{9,10},{10,1... | collective-permute-start | bytes 1658888 | tf_op jit(solution)/shard_map/ppermute | solution.py:322
  335.4 48.1 %all-gather.20.cloned.1.call-start = ((), (), s32[]{:S(2)}) async-start(), calls=%async_computation.18 | async-start | bytes 1966080 | tf_op jit(solution)/shard_map/all_gather | solution.py:33
  363.7 41.2 %all-gather.22.cloned.1.call-start = ((), (), s32[]{:S(2)}) async-start(), calls=%async_computation.20 | async-start | bytes 1966080 | tf_op jit(solution)/shard_map/all_gather | solution.py:33
  364.4 80.3 %reduce-scatter.23.cloned.1.call-start = ((), (), s32[]{:S(2)}) async-start(), calls=%async_computation.21 | async-start | bytes 1966080 | tf_op jit(solution)/shard_map/reduce_scatter | solution.py:37
  416.3 59.5 %reduce-scatter.21.cloned.1.call-start = ((), (), s32[]{:S(2)}) async-start(), calls=%async_computation.19 | async-start | bytes 1966080 | tf_op jit(solution)/shard_map/reduce_scatter | solution.py:37
  420.7 57.4 %copy-start.12 = (bf16[1,256,768]{2,1,0:T(8,128)(2,1)S(1)}, bf16[1,256,768]{2,1,0:T(8,128)(2,1)}, u32[]{:S(2)}) copy-start(bf16[1,256,768]{2,1,0:T(8,128)(2,1)} %param.27) | copy-start | bytes 1179652
  420.7 78.7 %all-gather.24.cloned.1.call-start = ((), (), s32[]{:S(2)}) async-start(), calls=%async_computation.22 | async-start | bytes 1966080 | tf_op jit(solution)/shard_map/all_gather | solution.py:33
  479.6 82.8 %reduce-scatter.25.cloned.1.call-start = ((), (), s32[]{:S(2)}) async-start(), calls=%async_computation.23 | async-start | bytes 1966080 | tf_op jit(solution)/shard_map/reduce_scatter | solution.py:37
  530.3 32.2 %copy-start.38 = (f32[768]{0:T(1024)S(1)}, f32[768]{0:T(1024)}, u32[]{:S(2)}) copy-start(f32[768]{0:T(1024)} %copy-done.37) | copy-start | bytes 9220
  530.3 32.2 %copy-start.47 = (f32[256]{0:T(256)S(1)}, f32[256]{0:T(256)}, u32[]{:S(2)}) copy-start(f32[256]{0:T(256)} %copy-done.46) | copy-start | bytes 3076
  530.3 34.1 %copy-start.81 = (f32[256]{0:T(256)S(1)}, f32[256]{0:T(256)}, u32[]{:S(2)}) copy-start(f32[256]{0:T(256)} %copy-done.80) | copy-start | bytes 3076
  530.3 34.1 %copy-start.73 = (f32[256]{0:T(256)S(1)}, f32[256]{0:T(256)}, u32[]{:S(2)}) copy-start(f32[256]{0:T(256)} %copy-done.72) | copy-start | bytes 3076
  534.1 32.3 %copy-start.83 = (f32[256]{0:T(256)S(1)}, f32[256]{0:T(256)}, u32[]{:S(2)}) copy-start(f32[256]{0:T(256)} %copy-done.82) | copy-start | bytes 3076
  534.2 54.9 %all-gather.26.cloned.1.call-start = ((), (), s32[]{:S(2)}) async-start(), calls=%async_computation.24 | async-start | bytes 1966080 | tf_op jit(solution)/shard_map/all_gather | solution.py:33
  569.2 59.6 %reduce-scatter.27.cloned.1.call-start = ((), (), s32[]{:S(2)}) async-start(), calls=%async_computation.25 | async-start | bytes 1966080 | tf_op jit(solution)/shard_map/reduce_scatter | solution.py:37
  596.6 32.2 %copy-start.29 = (f32[768]{0:T(1024)S(1)}, f32[768]{0:T(1024)}, u32[]{:S(2)}) copy-start(f32[768]{0:T(1024)} %copy-done.28) | copy-start | bytes 9220
  596.6 32.2 %copy-start.31 = (f32[768]{0:T(1024)S(1)}, f32[768]{0:T(1024)}, u32[]{:S(2)}) copy-start(f32[768]{0:T(1024)} %copy-done.30) | copy-start | bytes 9220
  596.6 32.2 %copy-start.43 = (f32[256]{0:T(256)S(1)}, f32[256]{0:T(256)}, u32[]{:S(2)}) copy-start(f32[256]{0:T(256)} %copy-done.42) | copy-start | bytes 3076
  596.6 34.2 %copy-start.79 = (f32[256]{0:T(256)S(1)}, f32[256]{0:T(256)}, u32[]{:S(2)}) copy-start(f32[256]{0:T(256)} %copy-done.78) | copy-start | bytes 3076
  596.6 34.2 %copy-start.49 = (f32[256]{0:T(256)S(1)}, f32[256]{0:T(256)}, u32[]{:S(2)}) copy-start(f32[256]{0:T(256)} %copy-done.48) | copy-start | bytes 3076
  600.5 68.2 %all-gather.28.cloned.1.call-start = ((), (), s32[]{:S(2)}) async-start(), calls=%async_computation.26 | async-start | bytes 1966080 | tf_op jit(solution)/shard_map/all_gather | solution.py:33
  643.2 15.1 %all-to-all-start.1 = ((bf16[192,4,192]{0,2,1:T(8,128)(2,1)}), bf16[192,4,192]{0,2,1:T(8,128)(2,1)S(1)}, u32[]{:S(2)}, u32[]{:S(2)}) async-start(bf16[192,4,192]{0,2,1:T(8,128)(2,1)} %bitcast.61), calls=%async_computation.9 | async-start | bytes 786432 | tf_op jit(solution)/shard_map/all_to_all | solution.py:147
  646.7 100.3 %reduce-scatter.33.cloned.1.call-start = ((), (), s32[]{:S(2)}) async-start(), calls=%async_computation.32 | async-start | bytes 3981312 | tf_op jit(solution)/shard_map/reduce_scatter | solution.py:173
  668.0 110.0 %reduce-scatter.29.cloned.1.call-start = ((), (), s32[]{:S(2)}) async-start(), calls=%async_computation.27 | async-start | bytes 1966080 | tf_op jit(solution)/shard_map/reduce_scatter | solution.py:37
  706.6 10.9 %all-to-all-start = ((bf16[192,4,192]{0,2,1:T(8,128)(2,1)}), bf16[192,4,192]{0,2,1:T(8,128)(2,1)S(1)}, u32[]{:S(2)}, u32[]{:S(2)}) async-start(bf16[192,4,192]{0,2,1:T(8,128)(2,1)} %bitcast.56), calls=%async_computation.8 | async-start | bytes 786432 | tf_op jit(solution)/shard_map/all_to_all | solution.py:147
  710.0 150.4 %reduce-scatter.31.cloned.1.call-start = ((), (), s32[]{:S(2)}) async-start(), calls=%async_computation.31 | async-start | bytes 3981312 | tf_op jit(solution)/shard_map/reduce_scatter | solution.py:173
  727.2 50.7 %copy-start.36 = (f32[768]{0:T(1024)S(1)}, f32[768]{0:T(1024)}, u32[]{:S(2)}) copy-start(f32[768]{0:T(1024)} %copy-done.35) | copy-start | bytes 9220
  727.3 50.7 %copy-start.45 = (f32[256]{0:T(256)S(1)}, f32[256]{0:T(256)}, u32[]{:S(2)}) copy-start(f32[256]{0:T(256)} %copy-done.44) | copy-start | bytes 3076
  727.3 52.0 %copy-start.77 = (f32[256]{0:T(256)S(1)}, f32[256]{0:T(256)}, u32[]{:S(2)}) copy-start(f32[256]{0:T(256)} %copy-done.76) | copy-start | bytes 3076
  727.3 52.0 %copy-start.55 = (f32[256]{0:T(256)S(1)}, f32[256]{0:T(256)}, u32[]{:S(2)}) copy-start(f32[256]{0:T(256)} %copy-done.54) | copy-start | bytes 3076
  727.3 53.6 %copy-start.61 = (f32[768]{0:T(1024)S(1)}, f32[768]{0:T(1024)}, u32[]{:S(2)}) copy-start(f32[768]{0:T(1024)} %get-tuple-element.32) | copy-start | bytes 9220
  727.3 53.6 %copy-start.60 = (f32[768]{0:T(1024)S(1)}, f32[768]{0:T(1024)}, u32[]{:S(2)}) copy-start(f32[768]{0:T(1024)} %get-tuple-element.14) | copy-start | bytes 9220
  727.3 53.6 %copy-start.59 = (f32[768]{0:T(1024)S(1)}, f32[768]{0:T(1024)}, u32[]{:S(2)}) copy-start(f32[768]{0:T(1024)} %get-tuple-element.22) | copy-start | bytes 9220
  727.3 53.6 %copy-start.70 = (f32[768]{0:T(1024)S(1)}, f32[768]{0:T(1024)}, u32[]{:S(2)}) copy-start(f32[768]{0:T(1024)} %get-tuple-element.29) | copy-start | bytes 9220
  727.4 155.0 %all-gather.32.cloned.1.call-start = ((), (), s32[]{:S(2)}) async-start(), calls=%async_computation.30 | async-start | bytes 2211840 | tf_op jit(solution)/shard_map/all_gather | solution.py:174
  747.0 259.1 %all-reduce.2.cloned.1.call-start = ((), (), s32[]{:S(2)}) async-start(), calls=%async_computation.28 | async-start | bytes 147456 | tf_op jit(solution)/shard_map/psum | solution.py:377
  781.7 248.6 %all-gather.30.cloned.1.call-start = ((), (), s32[]{:S(2)}) async-start(), calls=%async_computation.29 | async-start | bytes 2211840 | tf_op jit(solution)/shard_map/all_gather | solution.py:174
  (81 other events, 487.5 us)
Sparse Core Ops, SparseCore 0:
  68.1 20.8 all-gather.13
  150.4 26.7 reduce-scatter.14
  181.9 19.6 all-gather.15
  217.5 28.1 reduce-scatter.16
  252.3 20.0 all-gather.17
  335.6 25.6 reduce-scatter.18
  363.8 19.6 all-gather.19
  385.1 19.6 all-gather.21
  416.5 28.1 reduce-scatter.22
  447.6 28.1 reduce-scatter.20
  479.7 19.6 all-gather.23
  534.3 28.1 reduce-scatter.24
  569.3 19.6 all-gather.25
  600.6 28.1 reduce-scatter.26
  635.9 23.8 all-gather.27
  668.1 78.8 reduce-scatter.32
  750.1 27.7 reduce-scatter.28
  781.4 78.9 reduce-scatter.30
  862.0 20.2 all-gather.31
  887.7 118.3 all-reduce.1
  1007.7 22.6 all-gather.29
